TPU v7x, 32 devices: a whole 2x2x4 slice. The times are simulated.
32 devices in a mesh: row: 8 (over z, x), col: 4 (over y, core).
Axes of the slice: x: 2, y: 2, z: 4, core: 2. Of those that a mesh axis runs over, the one named last changes fastest.
Arguments:
- rhs: bfloat16 [32768, 256], P(('row', 'col')), may hold values from -6 to 6
- order: int32 [32, 1024], P(('row', 'col')), may hold values from 0 to 1023, each once within a row
- leaf_inverse: bfloat16 [64, 512, 512], P(('row', 'col')), may hold values from -1 to 2
- leaf_column_generator: bfloat16 [64, 512, 256], P(('row', 'col')), may hold values from -0.25 to 0.25
- factor_up: bfloat16 [32, 5, 256, 256], P(('row', 'col')), may hold values from -1 to 1
- downward_coupling_factors: bfloat16 [32, 5, 256, 256], P(('row', 'col')), may hold values from -1 to 2
Outputs:
- solution: bfloat16 [32768, 256], P(('row', 'col'))
All inputs are finite; a program needn't handle non-finite values.
Results may differ from a plain program's by a relative error of at most 0.015.
Values may be sent and summed in bfloat16 or wider, within the bound.
A program may use at most 64 MiB of HBM per device.

v0:
```python
import jax
import jax.numpy as jnp
from jax import lax
from jax.sharding import PartitionSpec as P


def from_partner(x, axis, bit):
    return lax.ppermute(x, axis, [(i, i ^ 1 << bit) for i in range(lax.axis_size(axis))])


def up_partner(value, level, col_bits):
    if level < col_bits:
        return from_partner(value, "col", level)
    return from_partner(value, "row", level - col_bits)


def down_partner(value, level, col_bits):
    if level < col_bits:
        return from_partner(value, "col", level)
    return from_partner(value, "row", level - col_bits)


def times(kernel_matrix, value):
    return jnp.dot(kernel_matrix, value, preferred_element_type=jnp.float32)


def times_transposed(kernel_matrix, value):
    return jnp.einsum("ji,jg->ig", kernel_matrix, value, preferred_element_type=jnp.float32)


def on_device(
    rhs, order, leaf_inverse, leaf_column_generator, factor_up, downward_coupling_factors
):
    positions = order[0]
    leaves = leaf_inverse.shape[0]
    leaf = leaf_inverse.shape[1]
    genes = rhs.shape[1]
    ordered = jnp.take(rhs, positions, axis=0)
    blocks = ordered.reshape(leaves, leaf, genes)
    eliminated_rows = jnp.einsum(
        "jab,jbg->jag", leaf_inverse, blocks, preferred_element_type=jnp.float32
    )
    elimination_portion = eliminated_rows.astype(jnp.bfloat16)
    solve_state = jnp.einsum(
        "dmq,dms->qs",
        leaf_column_generator,
        elimination_portion,
        preferred_element_type=jnp.float32,
    )
    up_mats = factor_up[0]
    down_mats = downward_coupling_factors[0]
    levels = up_mats.shape[0]
    col_bits = lax.axis_size("col").bit_length() - 1
    saved = []
    for level in range(levels):
        saved.append(solve_state)
        term = times(up_mats[level], solve_state.astype(jnp.bfloat16)).astype(jnp.bfloat16)
        partner_values = up_partner(term, level, col_bits)
        solve_state = term.astype(jnp.float32) + partner_values.astype(jnp.float32)
    top = solve_state
    for level in reversed(range(levels)):
        rounded = top.astype(jnp.bfloat16)
        own = times_transposed(up_mats[level], rounded)
        sent = times(down_mats[level], rounded).astype(jnp.bfloat16)
        partner_values = down_partner(sent, level, col_bits)
        top = saved[level] + 0.5 * (partner_values.astype(jnp.float32) - own)
    top_half = top.astype(jnp.bfloat16)
    back = jnp.einsum(
        "jar,rg->jag", leaf_column_generator, top_half, preferred_element_type=jnp.float32
    ).astype(jnp.bfloat16)
    solved = eliminated_rows - jnp.einsum(
        "jab,jbg->jag", leaf_inverse, back, preferred_element_type=jnp.float32
    )
    flat = solved.reshape(leaves * leaf, genes).astype(jnp.bfloat16)
    placed = jnp.zeros((leaves * leaf, genes), jnp.bfloat16)
    return placed.at[positions].set(flat)


def solution(mesh):
    in_specs = (
        P(("row", "col"), None),
        P(("row", "col"), None),
        P(("row", "col"), None, None),
        P(("row", "col"), None, None),
        P(("row", "col"), None, None, None),
        P(("row", "col"), None, None, None),
    )
    out_specs = P(("row", "col"), None)
    return jax.shard_map(
        on_device, mesh=mesh, in_specs=in_specs, out_specs=out_specs, check_vma=False
    )
```

profile of v0, /device:TPU:0, one launch (start us, length us, event | category | flops | bytes accessed | tf_op | source)
XLA Modules:
  0.0 71.0 jit_solution(436487173687526987)
XLA Ops:
  0.0 0.8 %compare_select_fusion = s32[1024,1]{0,1:T(1,128)S(1)} fusion(s32[1,1024]{1,0:T(1,128)} %param.7), kind=kLoop, calls=%fused_computation.88 | loop fusion | flops 3072 | bytes 8192 | tf_op jit(solution)/shard_map/select_n | solution.py:76
  0.8 0.5 broadcast.51
  1.3 0.7 reduce.3
  2.0 4.6 %gather_fusion = bf16[1024,256]{1,0:T(8,128)(2,1)S(1)} fusion(bf16[1024,256]{1,0:T(8,128)(2,1)} %param.6, s32[1024]{0:T(1024)S(1)} %broadcast_clamp_fusion), kind=kCustom, calls=%fused_computation | custom fusion | bytes 1052672 | tf_op jit(solution)/shard_map/jit(_take)/gather | solution.py:38
  6.8 0.5 fusion.15
  7.3 0.5 copy-done.2
  7.9 0.3 convolution_bitcast_fusion
  8.2 0.8 %copy-done.1 = bf16[1,5,256,256]{3,2,1,0:T(8,128)(2,1)S(1)} copy-done((bf16[1,5,256,256]{3,2,1,0:T(8,128)(2,1)S(1)}, bf16[1,5,256,256]{3,2,1,0:T(8,128)(2,1)}, u32[]{:S(2)}) %copy-start.1) | copy-done | bytes 655384
  9.2 0.5 collective-permute-start
  9.7 1.0 %collective-permute-done = bf16[256,256]{0,1:T(8,128)(2,1)S(1)} collective-permute-done((bf16[256,256]{0,1:T(8,128)(2,1)S(1)}, bf16[256,256]{0,1:T(8,128)(2,1)S(1)}, u32[]{:S(2)}, u32[]{:S(2)}) %collective-permute-start) | collective-permute-done | bytes 131104 | tf_op jit(solution)/shard_map/ppermute | solution.py:8
  10.9 2.9 %collective-permute-start.1 = (bf16[256,256]{0,1:T(8,128)(2,1)S(1)}, bf16[256,256]{0,1:T(8,128)(2,1)S(1)}, u32[]{:S(2)}, u32[]{:S(2)}) collective-permute-start(bf16[256,256]{0,1:T(8,128)(2,1)S(1)} %fusion.4), channel_id=1, source_target_pairs={{0,2},{1,3},{2,0},{3,1},{4,6},{5,7},{6,4},{7,5},{8,10},{9,11},{10,... | collective-permute-start | bytes 393224 | tf_op jit(solution)/shard_map/ppermute | solution.py:8
  13.9 3.8 %collective-permute-done.1 = bf16[256,256]{0,1:T(8,128)(2,1)S(1)} collective-permute-done((bf16[256,256]{0,1:T(8,128)(2,1)S(1)}, bf16[256,256]{0,1:T(8,128)(2,1)S(1)}, u32[]{:S(2)}, u32[]{:S(2)}) %collective-permute-start.1) | collective-permute-done | bytes 131104 | tf_op jit(solution)/shard_map/ppermute | solution.py:8
  17.7 0.2 fusion.5
  17.9 1.8 %collective-permute-start.2 = (bf16[256,256]{0,1:T(8,128)(2,1)S(1)}, bf16[256,256]{0,1:T(8,128)(2,1)S(1)}, u32[]{:S(2)}, u32[]{:S(2)}) collective-permute-start(bf16[256,256]{0,1:T(8,128)(2,1)S(1)} %fusion.5), channel_id=1, source_target_pairs={{0,4},{4,0},{8,12},{12,8},{16,20},{20,16},{24,28},{28,24},{1,5},{5... | collective-permute-start | bytes 393224 | tf_op jit(solution)/shard_map/ppermute | solution.py:8
  19.7 3.3 %collective-permute-done.2 = bf16[256,256]{0,1:T(8,128)(2,1)S(1)} collective-permute-done((bf16[256,256]{0,1:T(8,128)(2,1)S(1)}, bf16[256,256]{0,1:T(8,128)(2,1)S(1)}, u32[]{:S(2)}, u32[]{:S(2)}) %collective-permute-start.2) | collective-permute-done | bytes 131104 | tf_op jit(solution)/shard_map/ppermute | solution.py:8
  23.0 0.2 fusion.6
  23.2 1.8 %collective-permute-start.3 = (bf16[256,256]{0,1:T(8,128)(2,1)S(1)}, bf16[256,256]{0,1:T(8,128)(2,1)S(1)}, u32[]{:S(2)}, u32[]{:S(2)}) collective-permute-start(bf16[256,256]{0,1:T(8,128)(2,1)S(1)} %fusion.6), channel_id=1, source_target_pairs={{0,8},{4,12},{8,0},{12,4},{16,24},{20,28},{24,16},{28,20},{1,9},{5... | collective-permute-start | bytes 393224 | tf_op jit(solution)/shard_map/ppermute | solution.py:8
  25.0 3.2 %collective-permute-done.3 = bf16[256,256]{0,1:T(8,128)(2,1)S(1)} collective-permute-done((bf16[256,256]{0,1:T(8,128)(2,1)S(1)}, bf16[256,256]{0,1:T(8,128)(2,1)S(1)}, u32[]{:S(2)}, u32[]{:S(2)}) %collective-permute-start.3) | collective-permute-done | bytes 131104 | tf_op jit(solution)/shard_map/ppermute | solution.py:8
  28.5 3.0 %collective-permute-start.4 = (bf16[256,256]{0,1:T(8,128)(2,1)S(1)}, bf16[256,256]{0,1:T(8,128)(2,1)S(1)}, u32[]{:S(2)}, u32[]{:S(2)}) collective-permute-start(bf16[256,256]{0,1:T(8,128)(2,1)S(1)} %fusion.7), channel_id=1, source_target_pairs={{0,16},{4,20},{8,24},{12,28},{16,0},{20,4},{24,8},{28,12},{1,17},{... | collective-permute-start | bytes 393224 | tf_op jit(solution)/shard_map/ppermute | solution.py:8
  31.5 4.4 %collective-permute-done.4 = bf16[256,256]{0,1:T(8,128)(2,1)S(1)} collective-permute-done((bf16[256,256]{0,1:T(8,128)(2,1)S(1)}, bf16[256,256]{0,1:T(8,128)(2,1)S(1)}, u32[]{:S(2)}, u32[]{:S(2)}) %collective-permute-start.4) | collective-permute-done | bytes 131104 | tf_op jit(solution)/shard_map/ppermute | solution.py:8
  36.1 2.1 %collective-permute-start.5 = (bf16[256,256]{0,1:T(8,128)(2,1)S(1)}, bf16[256,256]{0,1:T(8,128)(2,1)S(1)}, u32[]{:S(2)}, u32[]{:S(2)}) collective-permute-start(bf16[256,256]{0,1:T(8,128)(2,1)S(1)} %fusion.8), channel_id=1, source_target_pairs={{0,16},{4,20},{8,24},{12,28},{16,0},{20,4},{24,8},{28,12},{1,17},{... | collective-permute-start | bytes 393224 | tf_op jit(solution)/shard_map/ppermute | solution.py:8
  38.2 3.8 %collective-permute-done.5 = bf16[256,256]{0,1:T(8,128)(2,1)S(1)} collective-permute-done((bf16[256,256]{0,1:T(8,128)(2,1)S(1)}, bf16[256,256]{0,1:T(8,128)(2,1)S(1)}, u32[]{:S(2)}, u32[]{:S(2)}) %collective-permute-start.5) | collective-permute-done | bytes 131104 | tf_op jit(solution)/shard_map/ppermute | solution.py:8
  42.5 5.1 %collective-permute-start.6 = (bf16[256,256]{0,1:T(8,128)(2,1)S(1)}, bf16[256,256]{0,1:T(8,128)(2,1)S(1)}, u32[]{:S(2)}, u32[]{:S(2)}) collective-permute-start(bf16[256,256]{0,1:T(8,128)(2,1)S(1)} %fusion.9), channel_id=1, source_target_pairs={{0,8},{4,12},{8,0},{12,4},{16,24},{20,28},{24,16},{28,20},{1,9},{5... | collective-permute-start | bytes 393224 | tf_op jit(solution)/shard_map/ppermute | solution.py:8
  47.6 2.9 %collective-permute-done.6 = bf16[256,256]{0,1:T(8,128)(2,1)S(1)} collective-permute-done((bf16[256,256]{0,1:T(8,128)(2,1)S(1)}, bf16[256,256]{0,1:T(8,128)(2,1)S(1)}, u32[]{:S(2)}, u32[]{:S(2)}) %collective-permute-start.6) | collective-permute-done | bytes 131104 | tf_op jit(solution)/shard_map/ppermute | solution.py:8
  51.0 1.6 %collective-permute-start.7 = (bf16[256,256]{0,1:T(8,128)(2,1)S(1)}, bf16[256,256]{0,1:T(8,128)(2,1)S(1)}, u32[]{:S(2)}, u32[]{:S(2)}) collective-permute-start(bf16[256,256]{0,1:T(8,128)(2,1)S(1)} %fusion.10), channel_id=1, source_target_pairs={{0,4},{4,0},{8,12},{12,8},{16,20},{20,16},{24,28},{28,24},{1,5},{5... | collective-permute-start | bytes 393224 | tf_op jit(solution)/shard_map/ppermute | solution.py:8
  52.5 3.5 %collective-permute-done.7 = bf16[256,256]{0,1:T(8,128)(2,1)S(1)} collective-permute-done((bf16[256,256]{0,1:T(8,128)(2,1)S(1)}, bf16[256,256]{0,1:T(8,128)(2,1)S(1)}, u32[]{:S(2)}, u32[]{:S(2)}) %collective-permute-start.7) | collective-permute-done | bytes 131104 | tf_op jit(solution)/shard_map/ppermute | solution.py:8
  56.4 1.6 %collective-permute-start.8 = (bf16[256,256]{0,1:T(8,128)(2,1)S(1)}, bf16[256,256]{0,1:T(8,128)(2,1)S(1)}, u32[]{:S(2)}, u32[]{:S(2)}) collective-permute-start(bf16[256,256]{0,1:T(8,128)(2,1)S(1)} %fusion.11), channel_id=1, source_target_pairs={{0,2},{1,3},{2,0},{3,1},{4,6},{5,7},{6,4},{7,5},{8,10},{9,11},{10,... | collective-permute-start | bytes 393224 | tf_op jit(solution)/shard_map/ppermute | solution.py:8
  58.0 3.5 %collective-permute-done.8 = bf16[256,256]{0,1:T(8,128)(2,1)S(1)} collective-permute-done((bf16[256,256]{0,1:T(8,128)(2,1)S(1)}, bf16[256,256]{0,1:T(8,128)(2,1)S(1)}, u32[]{:S(2)}, u32[]{:S(2)}) %collective-permute-start.8) | collective-permute-done | bytes 131104 | tf_op jit(solution)/shard_map/ppermute | solution.py:8
  62.0 0.9 %convolution_bitcast_fusion.1 = f32[256,256]{0,1:T(8,128)} fusion(bf16[256,256]{0,1:T(8,128)(2,1)S(1)} %add_convert_fusion.1, bf16[1,5,256,256]{3,2,1,0:T(8,128)(2,1)S(1)} %copy-done.1), kind=kOutput, calls=%fused_computation.8 | convolution fusion | flops 33554432 | bytes 524288 | tf_op jit(solution)/shard_map/ji,jg->ig/dot_general | solution.py:28
  62.9 0.6 collective-permute-done.9
  63.4 1.6 %fusion.2 = bf16[2,512,256]{1,2,0:T(8,128)(2,1)S(1)} fusion(f32[2,256,512]{2,1,0:T(8,128)S(1)} %fusion.15, bf16[2,512,512]{2,1,0:T(8,128)(2,1)S(1)} %copy-done, bf16[2,512,256]{2,1,0:T(8,128)(2,1)S(1)} %copy-done.2, f32[256,256]{0,1:T(8,128)S(1)} %convolution_bitcast_fusion, f32[256,256]{0,1:T(8,128)} %convolution_bitcast_fusion.1, ...), kind=kOutput, calls=%fused_computation.6 | convolution fusion | flops 403767296 | bytes 3801088 | tf_op jit(solution)/shard_map/jab,jbg->jag/dot_general | solution.py:71
  65.3 5.7 %scatter_custom_fusion = bf16[1024,256]{1,0:T(8,128)(2,1)} fusion(s32[1024]{0:T(1024)S(1)} %bitcast.126, bf16[1024,256]{1,0:T(8,128)(2,1)S(1)} %bitcast.124, bf16[]{:T(256)} %constant.6.clone.1), kind=kCustom, calls=%fused_computation.49 | custom fusion | bytes 524290 | tf_op jit(solution)/shard_map/scatter | solution.py:76
  (26 shorter events, 3.1 us)
Async XLA Ops:
  0.0 6.8 %copy-start = (bf16[2,512,512]{2,1,0:T(8,128)(2,1)S(1)}, bf16[2,512,512]{2,1,0:T(8,128)(2,1)}, u32[]{:S(2)}) copy-start(bf16[2,512,512]{2,1,0:T(8,128)(2,1)} %param.8) | copy-start | bytes 3145732
  0.0 1.3 %copy-start.4 = (s32[1,1024]{1,0:T(1,128)S(1)}, s32[1,1024]{1,0:T(1,128)}, u32[]{:S(2)}) copy-start(s32[1,1024]{1,0:T(1,128)} %param.7) | copy-start | bytes 12292
  6.8 1.0 %copy-start.2 = (bf16[2,512,256]{2,1,0:T(8,128)(2,1)S(1)}, bf16[2,512,256]{2,1,0:T(8,128)(2,1)}, u32[]{:S(2)}) copy-start(bf16[2,512,256]{2,1,0:T(8,128)(2,1)} %param.9) | copy-start | bytes 1572868
  7.9 1.1 %copy-start.1 = (bf16[1,5,256,256]{3,2,1,0:T(8,128)(2,1)S(1)}, bf16[1,5,256,256]{3,2,1,0:T(8,128)(2,1)}, u32[]{:S(2)}) copy-start(bf16[1,5,256,256]{3,2,1,0:T(8,128)(2,1)} %param.10) | copy-start | bytes 1966084
  9.2 1.5 %collective-permute-start = (bf16[256,256]{0,1:T(8,128)(2,1)S(1)}, bf16[256,256]{0,1:T(8,128)(2,1)S(1)}, u32[]{:S(2)}, u32[]{:S(2)}) collective-permute-start(bf16[256,256]{0,1:T(8,128)(2,1)S(1)} %fusion.3), channel_id=1, source_target_pairs={{0,1},{1,0},{2,3},{3,2},{4,5},{5,4},{6,7},{7,6},{8,9},{9,8},{10,11... | collective-permute-start | bytes 393224 | tf_op jit(solution)/shard_map/ppermute | solution.py:8
  10.9 6.7 %collective-permute-start.1 = (bf16[256,256]{0,1:T(8,128)(2,1)S(1)}, bf16[256,256]{0,1:T(8,128)(2,1)S(1)}, u32[]{:S(2)}, u32[]{:S(2)}) collective-permute-start(bf16[256,256]{0,1:T(8,128)(2,1)S(1)} %fusion.4), channel_id=1, source_target_pairs={{0,2},{1,3},{2,0},{3,1},{4,6},{5,7},{6,4},{7,5},{8,10},{9,11},{10,... | collective-permute-start | bytes 393224 | tf_op jit(solution)/shard_map/ppermute | solution.py:8
  17.9 17.9 %copy-start.3 = (bf16[1,5,256,256]{3,2,1,0:T(8,128)(2,1)S(1)}, bf16[1,5,256,256]{3,2,1,0:T(8,128)(2,1)}, u32[]{:S(2)}) copy-start(bf16[1,5,256,256]{3,2,1,0:T(8,128)(2,1)} %param.11) | copy-start | bytes 1966084
  17.9 5.1 %collective-permute-start.2 = (bf16[256,256]{0,1:T(8,128)(2,1)S(1)}, bf16[256,256]{0,1:T(8,128)(2,1)S(1)}, u32[]{:S(2)}, u32[]{:S(2)}) collective-permute-start(bf16[256,256]{0,1:T(8,128)(2,1)S(1)} %fusion.5), channel_id=1, source_target_pairs={{0,4},{4,0},{8,12},{12,8},{16,20},{20,16},{24,28},{28,24},{1,5},{5... | collective-permute-start | bytes 393224 | tf_op jit(solution)/shard_map/ppermute | solution.py:8
  23.2 5.0 %collective-permute-start.3 = (bf16[256,256]{0,1:T(8,128)(2,1)S(1)}, bf16[256,256]{0,1:T(8,128)(2,1)S(1)}, u32[]{:S(2)}, u32[]{:S(2)}) collective-permute-start(bf16[256,256]{0,1:T(8,128)(2,1)S(1)} %fusion.6), channel_id=1, source_target_pairs={{0,8},{4,12},{8,0},{12,4},{16,24},{20,28},{24,16},{28,20},{1,9},{5... | collective-permute-start | bytes 393224 | tf_op jit(solution)/shard_map/ppermute | solution.py:8
  28.5 7.3 %collective-permute-start.4 = (bf16[256,256]{0,1:T(8,128)(2,1)S(1)}, bf16[256,256]{0,1:T(8,128)(2,1)S(1)}, u32[]{:S(2)}, u32[]{:S(2)}) collective-permute-start(bf16[256,256]{0,1:T(8,128)(2,1)S(1)} %fusion.7), channel_id=1, source_target_pairs={{0,16},{4,20},{8,24},{12,28},{16,0},{20,4},{24,8},{28,12},{1,17},{... | collective-permute-start | bytes 393224 | tf_op jit(solution)/shard_map/ppermute | solution.py:8
  36.1 6.0 %collective-permute-start.5 = (bf16[256,256]{0,1:T(8,128)(2,1)S(1)}, bf16[256,256]{0,1:T(8,128)(2,1)S(1)}, u32[]{:S(2)}, u32[]{:S(2)}) collective-permute-start(bf16[256,256]{0,1:T(8,128)(2,1)S(1)} %fusion.8), channel_id=1, source_target_pairs={{0,16},{4,20},{8,24},{12,28},{16,0},{20,4},{24,8},{28,12},{1,17},{... | collective-permute-start | bytes 393224 | tf_op jit(solution)/shard_map/ppermute | solution.py:8
  42.5 8.1 %collective-permute-start.6 = (bf16[256,256]{0,1:T(8,128)(2,1)S(1)}, bf16[256,256]{0,1:T(8,128)(2,1)S(1)}, u32[]{:S(2)}, u32[]{:S(2)}) collective-permute-start(bf16[256,256]{0,1:T(8,128)(2,1)S(1)} %fusion.9), channel_id=1, source_target_pairs={{0,8},{4,12},{8,0},{12,4},{16,24},{20,28},{24,16},{28,20},{1,9},{5... | collective-permute-start | bytes 393224 | tf_op jit(solution)/shard_map/ppermute | solution.py:8
  51.0 5.0 %collective-permute-start.7 = (bf16[256,256]{0,1:T(8,128)(2,1)S(1)}, bf16[256,256]{0,1:T(8,128)(2,1)S(1)}, u32[]{:S(2)}, u32[]{:S(2)}) collective-permute-start(bf16[256,256]{0,1:T(8,128)(2,1)S(1)} %fusion.10), channel_id=1, source_target_pairs={{0,4},{4,0},{8,12},{12,8},{16,20},{20,16},{24,28},{28,24},{1,5},{5... | collective-permute-start | bytes 393224 | tf_op jit(solution)/shard_map/ppermute | solution.py:8
  56.4 5.0 %collective-permute-start.8 = (bf16[256,256]{0,1:T(8,128)(2,1)S(1)}, bf16[256,256]{0,1:T(8,128)(2,1)S(1)}, u32[]{:S(2)}, u32[]{:S(2)}) collective-permute-start(bf16[256,256]{0,1:T(8,128)(2,1)S(1)} %fusion.11), channel_id=1, source_target_pairs={{0,2},{1,3},{2,0},{3,1},{4,6},{5,7},{6,4},{7,5},{8,10},{9,11},{10,... | collective-permute-start | bytes 393224 | tf_op jit(solution)/shard_map/ppermute | solution.py:8
  61.9 1.5 %collective-permute-start.9 = (bf16[256,256]{0,1:T(8,128)(2,1)S(1)}, bf16[256,256]{0,1:T(8,128)(2,1)}, u32[]{:S(2)}, u32[]{:S(2)}) collective-permute-start(bf16[256,256]{0,1:T(8,128)(2,1)S(1)} %fusion.12), channel_id=1, source_target_pairs={{0,1},{1,0},{2,3},{3,2},{4,5},{5,4},{6,7},{7,6},{8,9},{9,8},{10,11... | collective-permute-start | bytes 393224 | tf_op jit(solution)/shard_map/ppermute | solution.py:8
where the time goes:
time: 71.3 us; the launch traced here: 71 us
  waiting for transfers between devices  30 us (42%)
  starting transfers between devices  20.5 us (29%)
  local copies, waits for them, and re-layouts  12.6 us (18%)
  matrix products  6.25 us (9%)
  other arithmetic  1.47 us (2%)
    ppermute x10, waiting for transfers between devices, from_partner(): lax.ppermute(x, axis, [(i, i ^ 1 << bit) for i in range(lax.axis_size(axi...  30 us
    ppermute x10, starting transfers between devices, from_partner(): lax.ppermute(x, axis, [(i, i ^ 1 << bit) for i in range(lax.axis_size(axi...  20.5 us
    scatter x1, local copies, waits for them, and re-layouts, on_device(): return placed.at[positions].set(flat)  5.72 us
    gather x2, local copies, waits for them, and re-layouts, on_device(): ordered = jnp.take(rhs, positions, axis=0)  4.78 us
    dot_general x10, matrix products, times(): return jnp.dot(kernel_matrix, value, preferred_element_type=jnp.float32)  2.19 us
    unnamed x11, local copies, waits for them, and re-layouts  1.86 us
    dot_general x5, matrix products, times_transposed(): jnp.einsum('ji,jg->ig', kernel_matrix, value, preferred_element_type=jnp....  1.69 us
    dot_general x1, matrix products, on_device(): jnp.einsum('jab,jbg->jag', leaf_inverse, back, preferred_element_type=jnp...  1.6 us
  transfers between devices with their start and end apart: 10, of which 10 were waited for; matrix products, arithmetic and copies ran while one was open for 1% of the time, Pallas kernels for 0%

commit v1 on v0

v1 whole, which is shorter than its diff:
```python
import functools

import jax
import jax.numpy as jnp
from jax import lax
from jax.experimental import pallas as pl
from jax.experimental.pallas import tpu as pltpu
from jax.sharding import PartitionSpec as P

CHUNKS = 4
LEAF_PARTS = 2


def nn(a, b):
    return lax.dot_general(a, b, (((1,), (0,)), ((), ())), preferred_element_type=jnp.float32)


def nt(a, b):
    return lax.dot_general(a, b, (((1,), (1,)), ((), ())), preferred_element_type=jnp.float32)


def flipped(index, bit):
    return index + bit * (1 - 2 * lax.rem(lax.div(index, bit), 2))


def kernel(
    col_bits,
    chunks,
    leaf_parts,
    order_ref,
    rhs_ref,
    inv_ref,
    gen_ref,
    up_ref,
    down_ref,
    out_ref,
    rhs_v,
    inv_v,
    gen_v,
    up_v,
    down_v,
    far_v,
    place,
    elim,
    states,
    flat,
    send,
    recv,
    load_sem,
    send_sem,
    recv_sem,
    far_sem,
):
    bf16, f32 = jnp.bfloat16, jnp.float32
    levels = up_v.shape[0]
    leaves, leaf, _ = inv_v.shape
    bins, genes = rhs_v.shape
    piece = genes // chunks
    row, col = lax.axis_index("row"), lax.axis_index("col")
    partners = []
    for level in range(levels):
        if level < col_bits:
            partners.append((row, flipped(col, 1 << level)))
        else:
            partners.append((flipped(row, 1 << (level - col_bits)), col))

    barrier = pltpu.get_barrier_semaphore()
    for partner in partners:
        pl.semaphore_signal(
            barrier, inc=1, device_id=partner, device_id_type=pl.DeviceIdType.MESH
        )

    loads = [
        pltpu.make_async_copy(source, target, load_sem.at[i])
        for i, (source, target) in enumerate(
            ((rhs_ref, rhs_v), (inv_ref, inv_v), (gen_ref, gen_v), (up_ref.at[0], up_v),
             (down_ref.at[0], down_v))
        )
    ]
    for load in loads:
        load.start()

    block = 128
    for start in range(0, bins, block):
        index = lax.broadcasted_iota(jnp.int32, (block, bins), 0) + start
        hit = index == order_ref[...]
        place[start : start + block, :] = jnp.where(hit, 1.0, 0.0).astype(bf16)

    pl.semaphore_wait(barrier, levels)

    far = pltpu.make_async_remote_copy(
        src_ref=down_ref.at[0, levels - 1],
        dst_ref=far_v,
        send_sem=far_sem.at[0],
        recv_sem=far_sem.at[1],
        device_id=partners[levels - 1],
        device_id_type=pl.DeviceIdType.MESH,
    )
    far.start()

    events = list(range(levels)) + list(reversed(range(levels - 1)))
    copies = {}

    def rows(c):
        return slice(c * piece, (c + 1) * piece)

    def start(event, c, value):
        send[event, rows(c), :] = value
        copy = pltpu.make_async_remote_copy(
            src_ref=send.at[event, pl.ds(c * piece, piece)],
            dst_ref=recv.at[event, pl.ds(c * piece, piece)],
            send_sem=send_sem.at[event, c],
            recv_sem=recv_sem.at[event, c],
            device_id=partners[events[event]],
            device_id_type=pl.DeviceIdType.MESH,
        )
        copy.start()
        copies[event, c] = copy

    part = genes // leaf_parts
    loads[0].wait()
    rhs_t = rhs_v[...].T
    for h in range(leaf_parts):
        span = slice(h * part, (h + 1) * part)
        state = None
        for j in range(leaves):
            ordered = nn(rhs_t[span, :], place[:, j * leaf : (j + 1) * leaf]).astype(bf16)
            if h == 0 and j == 0:
                loads[1].wait()
            value = nt(ordered, inv_v[j])
            elim[j, span, :] = value
            if h == 0 and j == 0:
                loads[2].wait()
            own = nn(value.astype(bf16), gen_v[j])
            state = own if state is None else state + own
        states[0, span, :] = state
        if h == 0:
            loads[3].wait()
        term = nt(state.astype(bf16), up_v[0]).astype(bf16)
        for c in range(chunks // leaf_parts):
            start(0, h * (chunks // leaf_parts) + c, term[c * piece : (c + 1) * piece, :])

    for level in range(1, levels):
        for c in range(chunks):
            copies[level - 1, c].wait_recv()
            state = send[level - 1, rows(c), :].astype(f32) + recv[level - 1, rows(c), :].astype(
                f32
            )
            states[level, rows(c), :] = state
            start(level, c, nt(state.astype(bf16), up_v[level]).astype(bf16))

    for event in range(levels, 2 * levels - 1):
        level = events[event]
        for c in range(chunks):
            copies[event - 1, c].wait_recv()
            came = recv[event - 1, rows(c), :].astype(f32)
            if event == levels:
                if c == 0:
                    loads[4].wait()
                    far.wait_recv()
                y = (send[event - 1, rows(c), :].astype(f32) + came).astype(bf16)
                coupled = nt(y, far_v[...]).astype(bf16).astype(f32)
                top = states[levels - 1, rows(c), :] + 0.5 * (coupled - nn(y, up_v[levels - 1]))
            else:
                top = states[level + 1, rows(c), :] + 0.5 * came
            y = top.astype(bf16)
            start(event, c, nt(y, down_v[level]).astype(bf16))
            states[level, rows(c), :] = states[level, rows(c), :] - 0.5 * nn(y, up_v[level])

    last = 2 * levels - 2
    for c in range(chunks):
        copies[last, c].wait_recv()
        top = states[0, rows(c), :] + 0.5 * recv[last, rows(c), :].astype(f32)
        y = top.astype(bf16)
        for j in range(leaves):
            back = nt(y, gen_v[j]).astype(bf16)
            solved = elim[j, rows(c), :] - nt(back, inv_v[j])
            flat[rows(c), j * leaf : (j + 1) * leaf] = solved.astype(bf16)
    out_ref[...] = nt(place[...], flat[...]).astype(bf16)

    for copy in copies.values():
        copy.wait_send()
    far.wait_send()


def on_device(
    rhs, order, leaf_inverse, leaf_column_generator, factor_up, downward_coupling_factors
):
    leaves, leaf, _ = leaf_inverse.shape
    rank = leaf_column_generator.shape[2]
    bins, genes = rhs.shape
    levels = factor_up.shape[1]
    col_bits = lax.axis_size("col").bit_length() - 1
    bf16, f32 = jnp.bfloat16, jnp.float32
    exchanges = 2 * levels - 1
    return pl.pallas_call(
        functools.partial(kernel, col_bits, CHUNKS, LEAF_PARTS),
        out_shape=jax.ShapeDtypeStruct((bins, genes), bf16),
        in_specs=[pl.BlockSpec(memory_space=pltpu.VMEM)] + [pl.BlockSpec(memory_space=pl.ANY)] * 5,
        out_specs=pl.BlockSpec(memory_space=pltpu.VMEM),
        scratch_shapes=[
            pltpu.VMEM((bins, genes), bf16),
            pltpu.VMEM((leaves, leaf, leaf), bf16),
            pltpu.VMEM((leaves, leaf, rank), bf16),
            pltpu.VMEM((levels, rank, rank), bf16),
            pltpu.VMEM((levels, rank, rank), bf16),
            pltpu.VMEM((rank, rank), bf16),
            pltpu.VMEM((bins, bins), bf16),
            pltpu.VMEM((leaves, genes, leaf), f32),
            pltpu.VMEM((levels, genes, rank), f32),
            pltpu.VMEM((genes, bins), bf16),
            pltpu.VMEM((exchanges, genes, rank), bf16),
            pltpu.VMEM((exchanges, genes, rank), bf16),
            pltpu.SemaphoreType.DMA((5,)),
            pltpu.SemaphoreType.DMA((exchanges, CHUNKS)),
            pltpu.SemaphoreType.DMA((exchanges, CHUNKS)),
            pltpu.SemaphoreType.DMA((2,)),
        ],
        compiler_params=pltpu.CompilerParams(
            collective_id=0, has_side_effects=True, vmem_limit_bytes=48 * 1024 * 1024
        ),
        cost_estimate=pl.CostEstimate(
            flops=2 * (2 * bins * bins * genes + 2 * bins * leaf * genes + 2 * bins * rank * genes
                       + 3 * levels * rank * rank * genes),
            bytes_accessed=4 * bins * genes + 2 * leaves * leaf * (leaf + rank)
            + 4 * levels * rank * rank,
            transcendentals=0,
        ),
    )(order, rhs, leaf_inverse, leaf_column_generator, factor_up, downward_coupling_factors)


def solution(mesh):
    in_specs = (
        P(("row", "col"), None),
        P(("row", "col"), None),
        P(("row", "col"), None, None),
        P(("row", "col"), None, None),
        P(("row", "col"), None, None, None),
        P(("row", "col"), None, None, None),
    )
    out_specs = P(("row", "col"), None)
    return jax.shard_map(
        on_device, mesh=mesh, in_specs=in_specs, out_specs=out_specs, check_vma=False
    )
```

time: 71.3 us -> 44.2 us (0.62)
  Pallas kernels: 0 us -> 36.8 us
  waiting for transfers between devices: 30 us -> 0 us
  starting transfers between devices: 20.5 us -> 0 us
  matrix products: 6.25 us -> 0 us
  local copies, waits for them, and re-layouts: 12.6 us -> 6.96 us
  other arithmetic: 1.47 us -> 0 us
    pallas_call x0 -> x1, Pallas kernels: none -> 36.8 us  [on_device(): pl.pallas_call(functools.partial(kernel, col_bits, CHUNKS, LEAF_PARTS), o...]
    ppermute x10 -> x0, waiting for transfers between devices: 30 us -> none  [from_partner(): lax.ppermute(x, axis, [(i, i ^ 1 << bit) for i in range(lax.axis_size(axi...]
    ppermute x10 -> x0, starting transfers between devices: 20.5 us -> none  [from_partner(): lax.ppermute(x, axis, [(i, i ^ 1 << bit) for i in range(lax.axis_size(axi...]
    dot_general x18 -> x0, matrix products: 6.25 us -> none  [the longest x10 2.19 us: times(): return jnp.dot(kernel_matrix, value, preferred_element_type=jnp.float32)]
    scatter x1 -> x0, local copies, waits for them, and re-layouts: 5.72 us -> none  [on_device(): return placed.at[positions].set(flat)]
    unnamed x11 -> x13, local copies, waits for them, and re-layouts: 1.86 us -> 6.96 us
    gather x2 -> x0, local copies, waits for them, and re-layouts: 4.78 us -> none  [on_device(): ordered = jnp.take(rhs, positions, axis=0)]
    select_n x1 -> x0, other arithmetic: 0.79 us -> none  [on_device(): return placed.at[positions].set(flat)]
  transfers between devices with their start and end apart: 10 -> 0, of which waited for: 10 -> 0; matrix products, arithmetic and copies ran while one was open for 1% -> 0% of each run, Pallas kernels for 0% -> 0%
where the time goes in v1:
time: 44.2 us; the launch traced here: 43.8 us
  Pallas kernels  36.8 us (83%)
  local copies, waits for them, and re-layouts  6.96 us (16%)
    pallas_call x1, Pallas kernels, on_device(): pl.pallas_call(functools.partial(kernel, col_bits, CHUNKS, LEAF_PARTS), o...  36.8 us
    unnamed x13, local copies, waits for them, and re-layouts  6.96 us

profile of v1, /device:TPU:0, one launch (start us, length us, event | category | flops | bytes accessed | tf_op | source)
XLA Modules:
  0.0 43.8 jit_solution(4735117224941656449)
XLA Ops:
  0.0 0.0 copy-start
  0.0 1.2 %copy-done = bf16[2,512,512]{2,1,0:T(8,128)(2,1)S(1)} copy-done((bf16[2,512,512]{2,1,0:T(8,128)(2,1)S(1)}, bf16[2,512,512]{2,1,0:T(8,128)(2,1)}, u32[]{:S(2)}) %copy-start) | copy-done | bytes 1048600
  1.2 0.0 copy-start.1
  1.2 1.1 %copy-done.1 = bf16[1,5,256,256]{3,2,1,0:T(8,128)(2,1)S(1)} copy-done((bf16[1,5,256,256]{3,2,1,0:T(8,128)(2,1)S(1)}, bf16[1,5,256,256]{3,2,1,0:T(8,128)(2,1)}, u32[]{:S(2)}) %copy-start.1) | copy-done | bytes 655384
  2.3 0.0 copy-start.2
  2.3 1.1 %copy-done.2 = bf16[1,5,256,256]{3,2,1,0:T(8,128)(2,1)S(1)} copy-done((bf16[1,5,256,256]{3,2,1,0:T(8,128)(2,1)S(1)}, bf16[1,5,256,256]{3,2,1,0:T(8,128)(2,1)}, u32[]{:S(2)}) %copy-start.2) | copy-done | bytes 655384
  3.4 0.0 copy-start.3
  3.4 1.0 %copy-done.3 = bf16[1024,256]{1,0:T(8,128)(2,1)S(1)} copy-done((bf16[1024,256]{1,0:T(8,128)(2,1)S(1)}, bf16[1024,256]{1,0:T(8,128)(2,1)}, u32[]{:S(2)}) %copy-start.3) | copy-done | bytes 524312
  4.4 0.0 copy-start.4
  4.4 1.0 %copy-done.4 = bf16[2,512,256]{2,1,0:T(8,128)(2,1)S(1)} copy-done((bf16[2,512,256]{2,1,0:T(8,128)(2,1)S(1)}, bf16[2,512,256]{2,1,0:T(8,128)(2,1)}, u32[]{:S(2)}) %copy-start.4) | copy-done | bytes 524312
  5.5 0.0 copy-start.5
  5.5 0.7 %copy-done.5 = s32[1,1024]{1,0:T(1,128)S(1)} copy-done((s32[1,1024]{1,0:T(1,128)S(1)}, s32[1,1024]{1,0:T(1,128)}, u32[]{:S(2)}) %copy-start.5) | copy-done | bytes 4120
  6.2 36.8 %shard_map.64 = bf16[1024,256]{1,0:T(8,128)(2,1)S(1)} custom-call(s32[1,1024]{1,0:T(1,128)S(1)} %copy-done.5, bf16[1024,256]{1,0:T(8,128)(2,1)S(1)} %copy-done.3, bf16[2,512,512]{2,1,0:T(8,128)(2,1)S(1)} %copy-done, bf16[2,512,256]{2,1,0:T(8,128)(2,1)S(1)} %copy-done.4, bf16[1,5,256,256]{3,2,1,0:T(8,128)(2,1)S(1)} %copy-done.1, ...), custom_call_target="tpu_custom_call" | custom-call | flops 2382364672 | bytes 3932160 | tf_op jit(solution)/shard_map/pallas_call | solution.py:196
  43.0 0.8 %copy.8 = bf16[1024,256]{1,0:T(8,128)(2,1)} copy(bf16[1024,256]{1,0:T(8,128)(2,1)S(1)} %shard_map.64) | data formatting | bytes 1048576
Async XLA Ops:
  0.0 1.2 %copy-start = (bf16[2,512,512]{2,1,0:T(8,128)(2,1)S(1)}, bf16[2,512,512]{2,1,0:T(8,128)(2,1)}, u32[]{:S(2)}) copy-start(bf16[2,512,512]{2,1,0:T(8,128)(2,1)} %inv_ref.1) | copy-start | bytes 3145732
  1.2 1.1 %copy-start.1 = (bf16[1,5,256,256]{3,2,1,0:T(8,128)(2,1)S(1)}, bf16[1,5,256,256]{3,2,1,0:T(8,128)(2,1)}, u32[]{:S(2)}) copy-start(bf16[1,5,256,256]{3,2,1,0:T(8,128)(2,1)} %up_ref.1) | copy-start | bytes 1966084
  2.3 1.1 %copy-start.2 = (bf16[1,5,256,256]{3,2,1,0:T(8,128)(2,1)S(1)}, bf16[1,5,256,256]{3,2,1,0:T(8,128)(2,1)}, u32[]{:S(2)}) copy-start(bf16[1,5,256,256]{3,2,1,0:T(8,128)(2,1)} %down_ref.1) | copy-start | bytes 1966084
  3.4 1.0 %copy-start.3 = (bf16[1024,256]{1,0:T(8,128)(2,1)S(1)}, bf16[1024,256]{1,0:T(8,128)(2,1)}, u32[]{:S(2)}) copy-start(bf16[1024,256]{1,0:T(8,128)(2,1)} %rhs_ref.1) | copy-start | bytes 1572868
  4.4 1.0 %copy-start.4 = (bf16[2,512,256]{2,1,0:T(8,128)(2,1)S(1)}, bf16[2,512,256]{2,1,0:T(8,128)(2,1)}, u32[]{:S(2)}) copy-start(bf16[2,512,256]{2,1,0:T(8,128)(2,1)} %gen_ref.1) | copy-start | bytes 1572868
  5.5 0.7 %copy-start.5 = (s32[1,1024]{1,0:T(1,128)S(1)}, s32[1,1024]{1,0:T(1,128)}, u32[]{:S(2)}) copy-start(s32[1,1024]{1,0:T(1,128)} %order_ref.1) | copy-start | bytes 12292

commit v2 on v1

--- a/solution.py
+++ b/solution.py
@@ -34,6 +34,7 @@
     up_ref,
     down_ref,
     out_ref,
+    order_v,
     rhs_v,
     inv_v,
     gen_v,
@@ -44,6 +45,7 @@
     elim,
     states,
     flat,
+    ys,
     send,
     recv,
     load_sem,
@@ -73,17 +75,18 @@
     loads = [
         pltpu.make_async_copy(source, target, load_sem.at[i])
         for i, (source, target) in enumerate(
-            ((rhs_ref, rhs_v), (inv_ref, inv_v), (gen_ref, gen_v), (up_ref.at[0], up_v),
-             (down_ref.at[0], down_v))
+            ((order_ref, order_v), (rhs_ref, rhs_v), (inv_ref, inv_v), (gen_ref, gen_v),
+             (up_ref.at[0], up_v), (down_ref.at[0], down_v))
         )
     ]
     for load in loads:
         load.start()
 
+    loads[0].wait()
     block = 128
     for start in range(0, bins, block):
         index = lax.broadcasted_iota(jnp.int32, (block, bins), 0) + start
-        hit = index == order_ref[...]
+        hit = index == order_v[...]
         place[start : start + block, :] = jnp.where(hit, 1.0, 0.0).astype(bf16)
 
     pl.semaphore_wait(barrier, levels)
@@ -118,7 +121,7 @@
         copies[event, c] = copy
 
     part = genes // leaf_parts
-    loads[0].wait()
+    loads[1].wait()
     rhs_t = rhs_v[...].T
     for h in range(leaf_parts):
         span = slice(h * part, (h + 1) * part)
@@ -126,16 +129,16 @@
         for j in range(leaves):
             ordered = nn(rhs_t[span, :], place[:, j * leaf : (j + 1) * leaf]).astype(bf16)
             if h == 0 and j == 0:
-                loads[1].wait()
+                loads[2].wait()
             value = nt(ordered, inv_v[j])
             elim[j, span, :] = value
             if h == 0 and j == 0:
-                loads[2].wait()
+                loads[3].wait()
             own = nn(value.astype(bf16), gen_v[j])
             state = own if state is None else state + own
         states[0, span, :] = state
         if h == 0:
-            loads[3].wait()
+            loads[4].wait()
         term = nt(state.astype(bf16), up_v[0]).astype(bf16)
         for c in range(chunks // leaf_parts):
             start(0, h * (chunks // leaf_parts) + c, term[c * piece : (c + 1) * piece, :])
@@ -156,7 +159,7 @@
             came = recv[event - 1, rows(c), :].astype(f32)
             if event == levels:
                 if c == 0:
-                    loads[4].wait()
+                    loads[5].wait()
                     far.wait_recv()
                 y = (send[event - 1, rows(c), :].astype(f32) + came).astype(bf16)
                 coupled = nt(y, far_v[...]).astype(bf16).astype(f32)
@@ -165,17 +168,20 @@
                 top = states[level + 1, rows(c), :] + 0.5 * came
             y = top.astype(bf16)
             start(event, c, nt(y, down_v[level]).astype(bf16))
-            states[level, rows(c), :] = states[level, rows(c), :] - 0.5 * nn(y, up_v[level])
+            ys[rows(c), :] = y
+        states[level] = states[level] - 0.5 * nn(ys[...], up_v[level])
 
     last = 2 * levels - 2
-    for c in range(chunks):
-        copies[last, c].wait_recv()
-        top = states[0, rows(c), :] + 0.5 * recv[last, rows(c), :].astype(f32)
+    for h in range(leaf_parts):
+        span = slice(h * part, (h + 1) * part)
+        for c in range(h * (chunks // leaf_parts), (h + 1) * (chunks // leaf_parts)):
+            copies[last, c].wait_recv()
+        top = states[0, span, :] + 0.5 * recv[last, span, :].astype(f32)
         y = top.astype(bf16)
         for j in range(leaves):
             back = nt(y, gen_v[j]).astype(bf16)
-            solved = elim[j, rows(c), :] - nt(back, inv_v[j])
-            flat[rows(c), j * leaf : (j + 1) * leaf] = solved.astype(bf16)
+            solved = elim[j, span, :] - nt(back, inv_v[j])
+            flat[span, j * leaf : (j + 1) * leaf] = solved.astype(bf16)
     out_ref[...] = nt(place[...], flat[...]).astype(bf16)
 
     for copy in copies.values():
@@ -196,9 +202,10 @@
     return pl.pallas_call(
         functools.partial(kernel, col_bits, CHUNKS, LEAF_PARTS),
         out_shape=jax.ShapeDtypeStruct((bins, genes), bf16),
-        in_specs=[pl.BlockSpec(memory_space=pltpu.VMEM)] + [pl.BlockSpec(memory_space=pl.ANY)] * 5,
+        in_specs=[pl.BlockSpec(memory_space=pltpu.HBM)] * 6,
         out_specs=pl.BlockSpec(memory_space=pltpu.VMEM),
         scratch_shapes=[
+            pltpu.VMEM((1, bins), jnp.int32),
             pltpu.VMEM((bins, genes), bf16),
             pltpu.VMEM((leaves, leaf, leaf), bf16),
             pltpu.VMEM((leaves, leaf, rank), bf16),
@@ -209,15 +216,16 @@
             pltpu.VMEM((leaves, genes, leaf), f32),
             pltpu.VMEM((levels, genes, rank), f32),
             pltpu.VMEM((genes, bins), bf16),
+            pltpu.VMEM((genes, rank), bf16),
             pltpu.VMEM((exchanges, genes, rank), bf16),
             pltpu.VMEM((exchanges, genes, rank), bf16),
-            pltpu.SemaphoreType.DMA((5,)),
+            pltpu.SemaphoreType.DMA((6,)),
             pltpu.SemaphoreType.DMA((exchanges, CHUNKS)),
             pltpu.SemaphoreType.DMA((exchanges, CHUNKS)),
             pltpu.SemaphoreType.DMA((2,)),
         ],
         compiler_params=pltpu.CompilerParams(
-            collective_id=0, has_side_effects=True, vmem_limit_bytes=48 * 1024 * 1024
+            collective_id=0, has_side_effects=True, vmem_limit_bytes=60 * 1024 * 1024
         ),
         cost_estimate=pl.CostEstimate(
             flops=2 * (2 * bins * bins * genes + 2 * bins * leaf * genes + 2 * bins * rank * genes

time: 44.2 us -> 38.3 us (0.87)
  local copies, waits for them, and re-layouts: 6.96 us -> 1.87 us
  Pallas kernels: 36.8 us -> 36.3 us
    unnamed x13 -> x1, local copies, waits for them, and re-layouts: 6.96 us -> 1.87 us
    pallas_call x1, Pallas kernels: 36.8 us -> 36.3 us  [on_device(): pl.pallas_call(functools.partial(kernel, col_bits, CHUNKS, LEAF_PARTS), o...]
where the time goes in v2:
time: 38.3 us; the launch traced here: 38.2 us
  Pallas kernels  36.3 us (95%)
  local copies, waits for them, and re-layouts  1.87 us (5%)
    pallas_call x1, Pallas kernels, on_device(): pl.pallas_call(functools.partial(kernel, col_bits, CHUNKS, LEAF_PARTS), o...  36.3 us
    unnamed x1, local copies, waits for them, and re-layouts  1.87 us

profile of v2, /device:TPU:0, one launch (start us, length us, event | category | flops | bytes accessed | tf_op | source)
XLA Modules:
  0.0 38.2 jit_solution(7465032968969606897)
XLA Ops:
  0.0 36.3 %shard_map.64 = bf16[1024,256]{1,0:T(8,128)(2,1)} custom-call(s32[1,1024]{1,0:T(1,128)} %order_ref.1, bf16[1024,256]{1,0:T(8,128)(2,1)} %rhs_ref.1, bf16[2,512,512]{2,1,0:T(8,128)(2,1)} %inv_ref.1, bf16[2,512,256]{2,1,0:T(8,128)(2,1)} %gen_ref.1, bf16[1,5,256,256]{3,2,1,0:T(8,128)(2,1)} %up_ref.1, bf16[1,5,256,256]{3,2,1,0:T(8,128)(2,1)} %down_ref.1), custom_call_target="tpu_custom_call" | custom-call | flops 2382364672 | bytes 3932160 | tf_op jit(solution)/shard_map/pallas_call | solution.py:202
  36.3 1.9 %copy.8 = bf16[1024,256]{1,0:T(8,128)(2,1)} copy(bf16[1024,256]{1,0:T(8,128)(2,1)} %shard_map.64) | data formatting | bytes 1048576

commit v3 on v2

--- a/solution.py
+++ b/solution.py
@@ -45,7 +45,6 @@
     elim,
     states,
     flat,
-    ys,
     send,
     recv,
     load_sem,
@@ -143,45 +142,51 @@
         for c in range(chunks // leaf_parts):
             start(0, h * (chunks // leaf_parts) + c, term[c * piece : (c + 1) * piece, :])
 
-    for level in range(1, levels):
-        for c in range(chunks):
-            copies[level - 1, c].wait_recv()
-            state = send[level - 1, rows(c), :].astype(f32) + recv[level - 1, rows(c), :].astype(
-                f32
-            )
-            states[level, rows(c), :] = state
-            start(level, c, nt(state.astype(bf16), up_v[level]).astype(bf16))
-
-    for event in range(levels, 2 * levels - 1):
+    last = 2 * levels - 2
+
+    def go_up(level, c):
+        copies[level - 1, c].wait_recv()
+        state = send[level - 1, rows(c), :].astype(f32) + recv[level - 1, rows(c), :].astype(f32)
+        states[level, rows(c), :] = state
+        start(level, c, nt(state.astype(bf16), up_v[level]).astype(bf16))
+
+    def go_down(event, c):
         level = events[event]
-        for c in range(chunks):
-            copies[event - 1, c].wait_recv()
-            came = recv[event - 1, rows(c), :].astype(f32)
-            if event == levels:
-                if c == 0:
-                    loads[5].wait()
-                    far.wait_recv()
-                y = (send[event - 1, rows(c), :].astype(f32) + came).astype(bf16)
-                coupled = nt(y, far_v[...]).astype(bf16).astype(f32)
-                top = states[levels - 1, rows(c), :] + 0.5 * (coupled - nn(y, up_v[levels - 1]))
-            else:
-                top = states[level + 1, rows(c), :] + 0.5 * came
-            y = top.astype(bf16)
-            start(event, c, nt(y, down_v[level]).astype(bf16))
-            ys[rows(c), :] = y
-        states[level] = states[level] - 0.5 * nn(ys[...], up_v[level])
-
-    last = 2 * levels - 2
-    for h in range(leaf_parts):
+        copies[event - 1, c].wait_recv()
+        came = recv[event - 1, rows(c), :].astype(f32)
+        if event == levels:
+            if c == 0:
+                loads[5].wait()
+                far.wait_recv()
+            y = (send[event - 1, rows(c), :].astype(f32) + came).astype(bf16)
+            coupled = nt(y, far_v[...]).astype(bf16).astype(f32)
+            top = states[levels - 1, rows(c), :] + 0.5 * (coupled - nn(y, up_v[levels - 1]))
+        else:
+            top = states[level + 1, rows(c), :] + 0.5 * came
+        y = top.astype(bf16)
+        start(event, c, nt(y, down_v[level]).astype(bf16))
+        states[level, rows(c), :] = states[level, rows(c), :] - 0.5 * nn(y, up_v[level])
+
+    def finish(h):
         span = slice(h * part, (h + 1) * part)
-        for c in range(h * (chunks // leaf_parts), (h + 1) * (chunks // leaf_parts)):
-            copies[last, c].wait_recv()
         top = states[0, span, :] + 0.5 * recv[last, span, :].astype(f32)
         y = top.astype(bf16)
         for j in range(leaves):
             back = nt(y, gen_v[j]).astype(bf16)
             solved = elim[j, span, :] - nt(back, inv_v[j])
             flat[span, j * leaf : (j + 1) * leaf] = solved.astype(bf16)
+
+    for slot in range(1, last + 1 + chunks):
+        for c in range(chunks):
+            event = slot - c
+            if 0 < event < levels:
+                go_up(event, c)
+            elif levels <= event <= last:
+                go_down(event, c)
+            elif event == last + 1:
+                copies[last, c].wait_recv()
+                if (c + 1) * piece % part == 0:
+                    finish(c * piece // part)
     out_ref[...] = nt(place[...], flat[...]).astype(bf16)
 
     for copy in copies.values():
@@ -216,7 +221,6 @@
             pltpu.VMEM((leaves, genes, leaf), f32),
             pltpu.VMEM((levels, genes, rank), f32),
             pltpu.VMEM((genes, bins), bf16),
-            pltpu.VMEM((genes, rank), bf16),
             pltpu.VMEM((exchanges, genes, rank), bf16),
             pltpu.VMEM((exchanges, genes, rank), bf16),
             pltpu.SemaphoreType.DMA((6,)),

time: 38.3 us -> 49.1 us (1.28); the launches traced: 38.2 us -> 48.3 us
  Pallas kernels: 36.3 us -> 46.4 us
    pallas_call x1, Pallas kernels: 36.3 us -> 46.4 us  [on_device(): pl.pallas_call(functools.partial(kernel, col_bits, CHUNKS, LEAF_PARTS), o...]
where the time goes in v3:
time: 49.1 us; the launch traced here: 48.3 us
  Pallas kernels  46.4 us (95%)
  local copies, waits for them, and re-layouts  1.87 us (4%)
    pallas_call x1, Pallas kernels, on_device(): pl.pallas_call(functools.partial(kernel, col_bits, CHUNKS, LEAF_PARTS), o...  46.4 us
    unnamed x1, local copies, waits for them, and re-layouts  1.87 us

profile of v3, /device:TPU:0, one launch (start us, length us, event | category | flops | bytes accessed | tf_op | source)
XLA Modules:
  0.0 48.3 jit_solution(6076609657480881220)
XLA Ops:
  0.0 46.4 %shard_map.64 = bf16[1024,256]{1,0:T(8,128)(2,1)} custom-call(s32[1,1024]{1,0:T(1,128)} %order_ref.1, bf16[1024,256]{1,0:T(8,128)(2,1)} %rhs_ref.1, bf16[2,512,512]{2,1,0:T(8,128)(2,1)} %inv_ref.1, bf16[2,512,256]{2,1,0:T(8,128)(2,1)} %gen_ref.1, bf16[1,5,256,256]{3,2,1,0:T(8,128)(2,1)} %up_ref.1, bf16[1,5,256,256]{3,2,1,0:T(8,128)(2,1)} %down_ref.1), custom_call_target="tpu_custom_call" | custom-call | flops 2382364672 | bytes 3932160 | tf_op jit(solution)/shard_map/pallas_call | solution.py:207
  46.4 1.9 %copy.8 = bf16[1024,256]{1,0:T(8,128)(2,1)} copy(bf16[1024,256]{1,0:T(8,128)(2,1)} %shard_map.64) | data formatting | bytes 1048576

commit v4 on v2

--- a/solution.py
+++ b/solution.py
@@ -7,7 +7,7 @@
 from jax.experimental.pallas import tpu as pltpu
 from jax.sharding import PartitionSpec as P
 
-CHUNKS = 4
+CHUNKS = 2
 LEAF_PARTS = 2
 
 

time: 38.3 us -> 40.7 us (1.063)
  Pallas kernels: 36.3 us -> 38.6 us
    pallas_call x1, Pallas kernels: 36.3 us -> 38.6 us  [on_device(): pl.pallas_call(functools.partial(kernel, col_bits, CHUNKS, LEAF_PARTS), o...]
where the time goes in v4:
time: 40.7 us; the launch traced here: 40.5 us
  Pallas kernels  38.6 us (95%)
  local copies, waits for them, and re-layouts  1.87 us (5%)
    pallas_call x1, Pallas kernels, on_device(): pl.pallas_call(functools.partial(kernel, col_bits, CHUNKS, LEAF_PARTS), o...  38.6 us
    unnamed x1, local copies, waits for them, and re-layouts  1.87 us

profile of v4, /device:TPU:0, one launch (start us, length us, event | category | flops | bytes accessed | tf_op | source)
XLA Modules:
  0.0 40.5 jit_solution(550500221154767135)
XLA Ops:
  0.0 38.6 %shard_map.64 = bf16[1024,256]{1,0:T(8,128)(2,1)} custom-call(s32[1,1024]{1,0:T(1,128)} %order_ref.1, bf16[1024,256]{1,0:T(8,128)(2,1)} %rhs_ref.1, bf16[2,512,512]{2,1,0:T(8,128)(2,1)} %inv_ref.1, bf16[2,512,256]{2,1,0:T(8,128)(2,1)} %gen_ref.1, bf16[1,5,256,256]{3,2,1,0:T(8,128)(2,1)} %up_ref.1, bf16[1,5,256,256]{3,2,1,0:T(8,128)(2,1)} %down_ref.1), custom_call_target="tpu_custom_call" | custom-call | flops 2382364672 | bytes 3932160 | tf_op jit(solution)/shard_map/pallas_call | solution.py:202
  38.6 1.9 %copy.8 = bf16[1024,256]{1,0:T(8,128)(2,1)} copy(bf16[1024,256]{1,0:T(8,128)(2,1)} %shard_map.64) | data formatting | bytes 1048576
